TPU v7x, 256 devices: a whole 4x4x8 slice. The times are simulated.
256 devices in a mesh: az: 16 (over x, y_lo, core), rad: 16 (over z, y_hi).
Axes of the slice: x: 4, y: 4 (y_hi: 2, y_lo: 2; y = y_hi * 2 + y_lo), z: 8, core: 2. Of those that a mesh axis runs over, the one named last changes fastest.
Arguments:
- density: float32 [16, 128, 4096], P(None, 'rad', 'az'), may hold values from 0.5 to 2
- velocity: float32 [3, 16, 128, 4096], P(None, None, 'rad', 'az'), may hold values from -1 to 1
- energy: float32 [16, 128, 4096], P(None, 'rad', 'az'), may hold values from 0.5 to 2
- shifts: int32 [128], P('rad'), may hold values from 0 to 4095
- fraction: float32 [128], P('rad'), may hold values from 0 to 1
Outputs:
- density_out: float32 [16, 128, 4096], P(None, 'rad', 'az')
- velocity_out: float32 [3, 16, 128, 4096], P(None, None, 'rad', 'az')
- energy_out: float32 [16, 128, 4096], P(None, 'rad', 'az')
All inputs are finite; a program needn't handle non-finite values.
Results may differ from a plain program's by a relative error of at most 0.0003.
Values sent between devices are 32-bit elements; how exact they have to be, the bound alone decides.
A program may use at most 128 MiB of HBM per device.

v0:
```python
import jax
import jax.numpy as jnp
from jax import lax
from jax.experimental import pallas as pl
from jax.experimental.pallas import tpu as pltpu
from jax.sharding import PartitionSpec as P

MESH = pl.DeviceIdType.MESH
AZ = 16
QUADS = 32
CHUNKS = 32
CELLS = 4096
STEPS = 2

VT, EN, VR, DE, VP = range(5)
EARLY, LATE = (VT, EN, VR), (DE, VP)
GROUPS = (EARLY, LATE)
SPANS = (pl.ds(0, 3), pl.ds(3, 2))
S_VP = 3


def owner(pair, half):
    return lax.div(pair, 2) * 4 + half * 2 + lax.rem(pair, 2)


def prev_cell(x, lane):
    x1 = pltpu.roll(x, 1, 1)
    return jnp.where(lane == 0, pltpu.roll(x1, 1, 0), x1)


def next_cell(x, lane):
    x1 = pltpu.roll(x, 127, 1)
    return jnp.where(lane == 127, pltpu.roll(x1, CHUNKS - 1, 0), x1)


def kernel(
    den_hbm, vel_hbm, ene_hbm, shift_hbm, frac_hbm,
    back,
    den_ref, vel_ref, ene_ref, shift_ref, frac_ref,
    stage, rows, s0, s1, f0, f1, speed, flux, blended, ostage,
    a_send, a_recv, h_send, h_recv, b_send, b_recv, l_sem, i_sem,
):
    a = lax.axis_index("az")
    rho = lax.axis_index("rad")
    x, half, core = lax.div(a, 4), lax.rem(lax.div(a, 2), 2), lax.rem(a, 2)
    pair = 2 * x + core
    quad = 2 * rho + half
    states, fresh = (s0, s1), (f0, f1)

    loads = [
        pltpu.make_async_copy(src, dst, i_sem.at[n])
        for n, (src, dst) in enumerate((
            (ene_hbm, ene_ref), (vel_hbm, vel_ref), (den_hbm, den_ref), (shift_hbm, shift_ref), (frac_hbm, frac_ref)
        ))
    ]
    for copy in loads:
        copy.start()

    peers = []
    for k in range(AZ):
        dx, dy, dc = k // 4, (k // 2) % 2, k % 2
        peers.append(lax.rem(x + dx, 4) * 4 + lax.rem(half + dy, 2) * 2 + lax.rem(core + dc, 2))

    barrier = pltpu.get_barrier_semaphore()
    for k in range(1, AZ):
        pl.semaphore_signal(barrier, inc=1, device_id={"az": peers[k], "rad": rho}, device_id_type=MESH)
    cross = lax.rem(quad + 2 * half - 1 + QUADS, QUADS)
    pl.semaphore_signal(
        barrier, inc=1, device_id={"az": owner(pair, lax.rem(cross, 2)), "rad": lax.div(cross, 2)}, device_id_type=MESH
    )

    inner_t, inner_r = pl.ds(1, 2), pl.ds(1, 4)
    for buf, span in ((s0, pl.ds(0, 3)), (s1, pl.ds(0, 3)), (f0, pl.ds(0, 5)), (f1, pl.ds(0, 5))):
        def clear(where):
            buf[where] = jnp.zeros_like(buf[where])

        pl.when(pair == 0)(lambda: clear((span, 0, inner_r)))
        pl.when(pair == 7)(lambda: clear((span, 3, inner_r)))
        pl.when(quad == 0)(lambda: clear((span, inner_t, 0)))
        pl.when(quad == QUADS - 1)(lambda: clear((span, inner_t, 5)))

    sources = {VT: vel_ref.at[2], EN: ene_ref, VR: vel_ref.at[1], DE: den_ref, VP: vel_ref.at[0]}

    def regroup(fields):
        def one(tp, _):
            for h in range(2):
                dest = owner(tp, h)
                for f in fields:
                    for c in range(2):
                        for t in range(2):
                            stage[dest, f, pl.ds(c * 8 + t * 4, 4), :] = sources[f][
                                2 * tp + t, pl.ds(4 * h, 4), pl.ds(128 * c, 128)
                            ]
            return 0

        lax.fori_loop(0, 8, one, 0)

    def to_rows(k, g):
        dest = peers[k]
        return pltpu.make_async_remote_copy(
            src_ref=stage.at[dest, SPANS[g]],
            dst_ref=rows.at[SPANS[g], pl.ds(pl.multiple_of(a * 16, 16), 16), :],
            send_sem=a_send.at[g, k],
            recv_sem=a_recv.at[g, k],
            device_id={"az": dest, "rad": rho},
            device_id_type=MESH,
        )

    def own_rows(g):
        return pltpu.make_async_copy(
            stage.at[a, SPANS[g]], rows.at[SPANS[g], pl.ds(pl.multiple_of(a * 16, 16), 16), :], l_sem.at[g]
        )

    for copy in loads:
        copy.wait()
    regroup(EARLY)
    pl.semaphore_wait(barrier, AZ)
    for k in range(1, AZ):
        to_rows(k, 0).start()
    own_rows(0).start()
    regroup(LATE)
    for k in range(1, AZ):
        to_rows(k, 1).start()
    own_rows(1).start()

    lane = lax.broadcasted_iota(jnp.int32, (CHUNKS, 128), 1)
    lane8 = lax.broadcasted_iota(jnp.int32, (8, 128), 1)

    t_up, t_dn = lax.rem(pair + 1, 8), lax.rem(pair + 7, 8)
    r_up, r_dn = lax.rem(quad + 1, QUADS), lax.rem(quad + QUADS - 1, QUADS)
    has_tup, has_tdn = pair < 7, pair > 0
    has_rup, has_rdn = quad < QUADS - 1, quad > 0
    id_tup = {"az": owner(t_up, half), "rad": rho}
    id_tdn = {"az": owner(t_dn, half), "rad": rho}
    id_rup = {"az": owner(pair, lax.rem(r_up, 2)), "rad": lax.div(r_up, 2)}
    id_rdn = {"az": owner(pair, lax.rem(r_dn, 2)), "rad": lax.div(r_dn, 2)}

    def halo(buf, t_fields, r_fields, slot):
        def one(src, dst, ident, d):
            return pltpu.make_async_remote_copy(
                src_ref=src, dst_ref=dst, send_sem=h_send.at[slot, d], recv_sem=h_recv.at[slot, d],
                device_id=ident, device_id_type=MESH,
            )

        return (
            (one(buf.at[t_fields, 2, inner_r], buf.at[t_fields, 0, inner_r], id_tup, 0), has_tup, has_tdn),
            (one(buf.at[t_fields, 1, inner_r], buf.at[t_fields, 3, inner_r], id_tdn, 1), has_tdn, has_tup),
            (one(buf.at[r_fields, inner_t, 4], buf.at[r_fields, inner_t, 0], id_rup, 2), has_rup, has_rdn),
            (one(buf.at[r_fields, inner_t, 1], buf.at[r_fields, inner_t, 5], id_rdn, 3), has_rdn, has_rup),
        )

    def each(copies, what):
        for copy, sends, gets in copies:
            @pl.when(gets if what == "wait_recv" else sends)
            def _():
                getattr(copy, what)()

    def eight(body):
        def one(i, _):
            body(i, lax.div(i, 4) + 1, lax.rem(i, 4) + 1)
            return 0

        lax.fori_loop(0, 8, one, 0)

    def unpack(fields):
        def one(i, t, r):
            for q in fields:
                value = rows[q, pl.ds(i, CHUNKS, stride=8), :]
                if q == DE:
                    f0[DE, t, r] = value
                else:
                    s0[S_VP if q == VP else q, t, r] = value

        eight(one)

    def to_blocks(k, g):
        dest = peers[k]
        return pltpu.make_async_remote_copy(
            src_ref=ostage.at[SPANS[g], pl.ds(pl.multiple_of(dest * 16, 16), 16), :],
            dst_ref=back.at[a, SPANS[g]],
            send_sem=b_send.at[g, k],
            recv_sem=b_recv.at[g, k],
            device_id={"az": dest, "rad": rho},
            device_id_type=MESH,
        )

    def own_blocks(g):
        return pltpu.make_async_copy(
            ostage.at[SPANS[g], pl.ds(pl.multiple_of(a * 16, 16), 16), :], back.at[a, SPANS[g]], l_sem.at[2 + g]
        )

    plans = [
        (
            halo(states[step], pl.ds(0, 2), pl.ds(1, 2), 3 * step),
            halo(fresh[step], SPANS[1], SPANS[1], 3 * step + 1),
            halo(fresh[step], SPANS[0], SPANS[0], 3 * step + 2),
        )
        for step in range(STEPS)
    ]

    def along_azimuth(f, i, t, r, fields):
        p_lo = speed[i]
        for q in fields:
            v = f[q, t, r]
            low = p_lo * jnp.where(p_lo > 0, prev_cell(v, lane), v)
            flux[q, i] = next_cell(low, lane) - low

    def face(f, u, below, above):
        s = f[(u,) + below] + f[(u,) + above]
        up = s > 0
        return lambda q: s * jnp.where(up, f[(q,) + below], f[(q,) + above])

    for step in range(STEPS):
        s, f = states[step], fresh[step]
        first, late, early = plans[step]

        if step == 0:
            for k in range(1, AZ):
                to_rows(k, 0).wait_recv()
            own_rows(0).wait()
            unpack(EARLY)
            each(first, "start")
            for k in range(1, AZ):
                to_rows(k, 1).wait_recv()
            own_rows(1).wait()
            unpack(LATE)

        def source_azimuth(i, t, r):
            den = f[DE, t, r]
            k = 0.01 / jnp.where(den > 0, den, 1.0)
            e = s[EN, t, r]
            vp = s[S_VP, t, r]
            new = vp - k * (next_cell(e, lane) - prev_cell(e, lane))
            f[VP, t, r] = new
            flux[VT, i] = k
            flux[EN, i] = next_cell(vp, lane) - prev_cell(vp, lane)
            speed[i] = new + prev_cell(new, lane)

        eight(source_azimuth)
        each(late, "start")

        def azimuth_late(i, t, r):
            along_azimuth(f, i, t, r, LATE)

        eight(azimuth_late)
        each(first, "wait_recv")

        def source_rest(i, t, r):
            k = flux[VT, i]
            e = s[EN, t, r]
            f[VR, t, r] = s[VR, t, r] - k * (s[EN, t, r + 1] - s[EN, t, r - 1])
            f[VT, t, r] = s[VT, t, r] - k * (s[EN, t + 1, r] - s[EN, t - 1, r])
            div = (
                flux[EN, i]
                + (s[VR, t, r + 1] - s[VR, t, r - 1])
                + (s[VT, t + 1, r] - s[VT, t - 1, r])
            )
            f[EN, t, r] = e - 0.01 * e * div

        eight(source_rest)
        each(early, "start")

        def azimuth_early(i, t, r):
            along_azimuth(f, i, t, r, EARLY)

        eight(azimuth_early)

        def inner_radius(n, _):
            t, r = lax.div(n, 3), lax.rem(n, 3)
            one = face(f, VR, (t + 1, r + 1), (t + 1, r + 2))
            for q in range(5):
                v = one(q)
                flux[q, 4 * t + r] += v
                flux[q, 4 * t + r + 1] -= v
            return 0

        lax.fori_loop(0, 6, inner_radius, 0)

        def inner_theta(r, _):
            one = face(f, VT, (1, r + 1), (2, r + 1))
            for q in range(5):
                v = one(q)
                flux[q, r] += v
                flux[q, 4 + r] -= v
            return 0

        lax.fori_loop(0, 4, inner_theta, 0)

        each(late, "wait_recv")
        each(early, "wait_recv")

        for g, fields in enumerate(GROUPS):
            def outer_radius(t, _):
                low = face(f, VR, (t + 1, 0), (t + 1, 1))
                high = face(f, VR, (t + 1, 4), (t + 1, 5))
                for q in fields:
                    flux[q, 4 * t] -= low(q)
                    flux[q, 4 * t + 3] += high(q)
                return 0

            lax.fori_loop(0, 2, outer_radius, 0)

            def outer_theta(r, _):
                low = face(f, VT, (0, r + 1), (1, r + 1))
                high = face(f, VT, (2, r + 1), (3, r + 1))
                for q in fields:
                    flux[q, r] -= low(q)
                    flux[q, 4 + r] += high(q)
                return 0

            lax.fori_loop(0, 4, outer_theta, 0)

            def blend(i, t, r):
                w = frac_ref[half * 4 + r - 1]
                for q in fields:
                    moved = f[q, t, r] - 0.025 * flux[q, i]
                    b = (1.0 - w) * moved + w * prev_cell(moved, lane)
                    blended[q, i, pl.ds(0, CHUNKS), :] = b
                    blended[q, i, pl.ds(CHUNKS, 8), :] = b[:8]

            eight(blend)

            def rotate(i, t, r):
                ahead = lax.rem(CELLS - shift_ref[half * 4 + r - 1], CELLS)
                whole, part = lax.div(ahead, 128), lax.rem(ahead, 128)
                back_by = lax.rem(128 - part, 128)
                for q in fields:
                    for m in range(4):
                        near = blended[q, i, pl.ds(lax.rem(whole + 8 * m, CHUNKS), 8), :]
                        far = blended[q, i, pl.ds(lax.rem(whole + 8 * m + 1, CHUNKS), 8), :]
                        out = jnp.where(
                            lane8 < 128 - part, pltpu.roll(near, back_by, 1), pltpu.roll(far, back_by, 1)
                        )
                        if step == STEPS - 1:
                            ostage[q, pl.ds(64 * m + i, 8, stride=8), :] = out
                        elif q == DE:
                            f1[DE, t, r, pl.ds(8 * m, 8), :] = out
                        else:
                            s1[S_VP if q == VP else q, t, r, pl.ds(8 * m, 8), :] = out

            eight(rotate)
            if step == STEPS - 1:
                for k in range(1, AZ):
                    to_blocks(k, g).start()
                own_blocks(g).start()
            elif g == 0:
                each(plans[step + 1][0], "start")

    for step in range(STEPS):
        for copies in plans[step]:
            each(copies, "wait_send")
    for g in range(2):
        for k in range(1, AZ):
            to_rows(k, g).wait_send()
            to_blocks(k, g).wait_send()
    for g in range(2):
        own_blocks(g).wait()
        for k in range(1, AZ):
            to_blocks(k, g).wait_recv()


def write_out(back, den_hbm, vel_hbm, ene_hbm, blocks, den_out, vel_out, ene_out, in_sem, out_sem):
    targets = {
        VT: (vel_out.at[2], vel_hbm.at[2]), EN: (ene_out, ene_hbm), VR: (vel_out.at[1], vel_hbm.at[1]),
        DE: (den_out, den_hbm), VP: (vel_out.at[0], vel_hbm.at[0]),
    }
    reads = [pltpu.make_async_copy(back.at[:, q], blocks.at[:, q], in_sem.at[q]) for q in range(5)]
    for copy in reads:
        copy.start()
    writes = []
    for q in range(5):
        reads[q].wait()
        dst = targets[q][0]

        def one(tp, _):
            for h in range(2):
                src = owner(tp, h)
                for c in range(2):
                    for t in range(2):
                        dst[2 * tp + t, pl.ds(4 * h, 4), pl.ds(128 * c, 128)] = blocks[
                            src, q, pl.ds(c * 8 + t * 4, 4), :
                        ]
            return 0

        lax.fori_loop(0, 8, one, 0)
        writes.append(pltpu.make_async_copy(*targets[q], out_sem.at[q]))
        writes[-1].start()
    for copy in writes:
        copy.wait()


def shards(density, velocity, energy, shifts, fraction):
    hbm = pl.BlockSpec(memory_space=pl.ANY)
    f32 = jnp.float32
    limit = 60 * 1024 * 1024
    block = (AZ, 5, 16, 128)
    dma = pltpu.SemaphoreType.DMA
    fields = [pltpu.VMEM(v.shape, f32) for v in (density, velocity, energy)]
    back = pl.pallas_call(
        kernel,
        out_shape=jax.ShapeDtypeStruct(block, f32),
        in_specs=[hbm] * 5,
        out_specs=hbm,
        scratch_shapes=fields + [
            pltpu.SMEM(shifts.shape, jnp.int32),
            pltpu.SMEM(fraction.shape, f32),
            pltpu.VMEM(block, f32),
            pltpu.VMEM((5, 256, 128), f32),
            pltpu.VMEM((4, 4, 6, CHUNKS, 128), f32),
            pltpu.VMEM((4, 4, 6, CHUNKS, 128), f32),
            pltpu.VMEM((5, 4, 6, CHUNKS, 128), f32),
            pltpu.VMEM((5, 4, 6, CHUNKS, 128), f32),
            pltpu.VMEM((8, CHUNKS, 128), f32),
            pltpu.VMEM((5, 8, CHUNKS, 128), f32),
            pltpu.VMEM((5, 8, CHUNKS + 8, 128), f32),
            pltpu.VMEM((5, 256, 128), f32),
            dma((2, AZ)),
            dma((2, AZ)),
            dma((3 * STEPS, 4)),
            dma((3 * STEPS, 4)),
            dma((2, AZ)),
            dma((2, AZ)),
            dma((4,)),
            dma((5,)),
        ],
        compiler_params=pltpu.CompilerParams(collective_id=0, has_side_effects=True, vmem_limit_bytes=limit),
    )(density, velocity, energy, shifts, fraction)
    return pl.pallas_call(
        write_out,
        out_shape=tuple(jax.ShapeDtypeStruct(v.shape, f32) for v in (density, velocity, energy)),
        in_specs=[hbm],
        out_specs=(hbm,) * 3,
        scratch_shapes=[pltpu.VMEM(block, f32)] + fields + [dma((5,)), dma((5,))],
        compiler_params=pltpu.CompilerParams(vmem_limit_bytes=limit),
    )(back)


def solution(mesh):
    placed = (
        P(None, "rad", "az"),
        P(None, None, "rad", "az"),
        P(None, "rad", "az"),
        P("rad"),
        P("rad"),
    )
    return jax.shard_map(
        shards,
        mesh=mesh,
        in_specs=placed,
        out_specs=(P(None, "rad", "az"), P(None, None, "rad", "az"), P(None, "rad", "az")),
        check_vma=False,
    )
```

profile of v0, /device:TPU:1, one launch (start us, length us, event | category | flops | bytes accessed | tf_op | source)
XLA Modules:
  0.0 53.5 jit_solution(16208854932753301301)
XLA Ops:
  0.6 50.8 %shard_map.76.back = f32[16,5,16,128]{3,2,1,0:T(8,128)} custom-call(f32[16,8,256]{2,1,0:T(8,128)} %den_hbm.1, f32[3,16,8,256]{3,2,1,0:T(8,128)} %vel_hbm.1, f32[16,8,256]{2,1,0:T(8,128)} %ene_hbm.1, s32[8]{0:T(128)} %shift_hbm.1, f32[8]{0:T(128)} %frac_hbm.1), custom_call_target="tpu_custom_call" | custom-call | tf_op jit(solution)/shard_map/pallas_call | solution.py:399
  51.5 2.1 %shard_map.77 = (f32[16,8,256]{2,1,0:T(8,128)}, f32[3,16,8,256]{3,2,1,0:T(8,128)}, f32[16,8,256]{2,1,0:T(8,128)}) custom-call(f32[16,5,16,128]{3,2,1,0:T(8,128)} %shard_map.76.back), custom_call_target="tpu_custom_call" | custom-call | tf_op jit(solution)/shard_map/pallas_call | solution.py:428
where the time goes:
time: 53.7 us; the launch traced here: 53.5 us
  Pallas kernels  52.9 us (99%)
  between operations  0.64 us (1%)
    pallas_call x1, Pallas kernels, shards(): pl.pallas_call(kernel, out_shape=jax.ShapeDtypeStruct(block, f32), in_spe...  50.8 us
    pallas_call x1, Pallas kernels, shards(): pl.pallas_call(write_out, out_shape=tuple((jax.ShapeDtypeStruct(v.shape,...  2.05 us

commit v1 on v0

--- a/solution.py
+++ b/solution.py
@@ -17,6 +17,8 @@
 GROUPS = (EARLY, LATE)
 SPANS = (pl.ds(0, 3), pl.ds(3, 2))
 S_VP = 3
+UNROLL = 8
+ORDER = (8, 4, 12, 2, 9, 5, 13, 3, 10, 6, 14, 1, 11, 7, 15)
 
 
 def owner(pair, half):
@@ -115,11 +117,11 @@
         copy.wait()
     regroup(EARLY)
     pl.semaphore_wait(barrier, AZ)
-    for k in range(1, AZ):
+    for k in ORDER:
         to_rows(k, 0).start()
     own_rows(0).start()
     regroup(LATE)
-    for k in range(1, AZ):
+    for k in ORDER:
         to_rows(k, 1).start()
     own_rows(1).start()
 
@@ -155,12 +157,12 @@
             def _():
                 getattr(copy, what)()
 
-    def eight(body):
+    def eight(body, unroll=1):
         def one(i, _):
             body(i, lax.div(i, 4) + 1, lax.rem(i, 4) + 1)
             return 0
 
-        lax.fori_loop(0, 8, one, 0)
+        lax.fori_loop(0, 8, one, 0, unroll=unroll)
 
     def unpack(fields):
         def one(i, t, r):
@@ -236,7 +238,7 @@
             flux[EN, i] = next_cell(vp, lane) - prev_cell(vp, lane)
             speed[i] = new + prev_cell(new, lane)
 
-        eight(source_azimuth)
+        eight(source_azimuth, UNROLL)
         each(late, "start")
 
         def azimuth_late(i, t, r):
@@ -257,7 +259,7 @@
             )
             f[EN, t, r] = e - 0.01 * e * div
 
-        eight(source_rest)
+        eight(source_rest, UNROLL)
         each(early, "start")
 
         def azimuth_early(i, t, r):
@@ -289,7 +291,9 @@
         each(late, "wait_recv")
         each(early, "wait_recv")
 
-        for g, fields in enumerate(GROUPS):
+        for g in ((0, 1) if step < STEPS - 1 else (1, 0)):
+            fields = GROUPS[g]
+
             def outer_radius(t, _):
                 low = face(f, VR, (t + 1, 0), (t + 1, 1))
                 high = face(f, VR, (t + 1, 4), (t + 1, 5))
@@ -310,27 +314,29 @@
 
             lax.fori_loop(0, 4, outer_theta, 0)
 
-            def blend(i, t, r):
-                w = frac_ref[half * 4 + r - 1]
+            def finish(i, t, r):
                 for q in fields:
                     moved = f[q, t, r] - 0.025 * flux[q, i]
-                    b = (1.0 - w) * moved + w * prev_cell(moved, lane)
-                    blended[q, i, pl.ds(0, CHUNKS), :] = b
-                    blended[q, i, pl.ds(CHUNKS, 8), :] = b[:8]
-
-            eight(blend)
+                    blended[q, i, pl.ds(0, CHUNKS), :] = moved
+                    blended[q, i, pl.ds(CHUNKS, 8), :] = moved[:8]
+
+            eight(finish, UNROLL)
 
             def rotate(i, t, r):
-                ahead = lax.rem(CELLS - shift_ref[half * 4 + r - 1], CELLS)
-                whole, part = lax.div(ahead, 128), lax.rem(ahead, 128)
-                back_by = lax.rem(128 - part, 128)
+                w = frac_ref[half * 4 + r - 1]
+                shift = shift_ref[half * 4 + r - 1]
+                views = []
+                for back_cells in (0, 1):
+                    ahead = lax.rem(2 * CELLS - shift - back_cells, CELLS)
+                    views.append((lax.div(ahead, 128), lax.rem(ahead, 128)))
                 for q in fields:
                     for m in range(4):
-                        near = blended[q, i, pl.ds(lax.rem(whole + 8 * m, CHUNKS), 8), :]
-                        far = blended[q, i, pl.ds(lax.rem(whole + 8 * m + 1, CHUNKS), 8), :]
-                        out = jnp.where(
-                            lane8 < 128 - part, pltpu.roll(near, back_by, 1), pltpu.roll(far, back_by, 1)
-                        )
+                        parts = []
+                        for whole, part in views:
+                            near = blended[q, i, pl.ds(lax.rem(whole + 8 * m, CHUNKS), 8), :]
+                            far = blended[q, i, pl.ds(lax.rem(whole + 8 * m + 1, CHUNKS), 8), :]
+                            parts.append(pltpu.roll(jnp.where(lane8 < part, far, near), lax.rem(128 - part, 128), 1))
+                        out = (1.0 - w) * parts[0] + w * parts[1]
                         if step == STEPS - 1:
                             ostage[q, pl.ds(64 * m + i, 8, stride=8), :] = out
                         elif q == DE:
@@ -338,9 +344,9 @@
                         else:
                             s1[S_VP if q == VP else q, t, r, pl.ds(8 * m, 8), :] = out
 
-            eight(rotate)
+            eight(rotate, UNROLL)
             if step == STEPS - 1:
-                for k in range(1, AZ):
+                for k in ORDER:
                     to_blocks(k, g).start()
                 own_blocks(g).start()
             elif g == 0:

time: 53.7 us -> 50.2 us (0.935)
  Pallas kernels: 52.9 us -> 49.4 us
    pallas_call x1, Pallas kernels: 50.8 us -> 47.3 us  [shards(): pl.pallas_call(kernel, out_shape=jax.ShapeDtypeStruct(block, f32), in_spe...]
where the time goes in v1:
time: 50.2 us; the launch traced here: 50 us
  Pallas kernels  49.4 us (98%)
  between operations  0.64 us (1%)
    pallas_call x1, Pallas kernels, shards(): pl.pallas_call(kernel, out_shape=jax.ShapeDtypeStruct(block, f32), in_spe...  47.3 us
    pallas_call x1, Pallas kernels, shards(): pl.pallas_call(write_out, out_shape=tuple((jax.ShapeDtypeStruct(v.shape,...  2.05 us

profile of v1, /device:TPU:1, one launch (start us, length us, event | category | flops | bytes accessed | tf_op | source)
XLA Modules:
  0.0 50.0 jit_solution(3388909926049909435)
XLA Ops:
  0.6 47.3 %shard_map.76.back = f32[16,5,16,128]{3,2,1,0:T(8,128)} custom-call(f32[16,8,256]{2,1,0:T(8,128)} %den_hbm.1, f32[3,16,8,256]{3,2,1,0:T(8,128)} %vel_hbm.1, f32[16,8,256]{2,1,0:T(8,128)} %ene_hbm.1, s32[8]{0:T(128)} %shift_hbm.1, f32[8]{0:T(128)} %frac_hbm.1), custom_call_target="tpu_custom_call" | custom-call | tf_op jit(solution)/shard_map/pallas_call | solution.py:405
  48.0 2.1 %shard_map.77 = (f32[16,8,256]{2,1,0:T(8,128)}, f32[3,16,8,256]{3,2,1,0:T(8,128)}, f32[16,8,256]{2,1,0:T(8,128)}) custom-call(f32[16,5,16,128]{3,2,1,0:T(8,128)} %shard_map.76.back), custom_call_target="tpu_custom_call" | custom-call | tf_op jit(solution)/shard_map/pallas_call | solution.py:434

commit v2 on v1

--- a/solution.py
+++ b/solution.py
@@ -12,8 +12,8 @@
 CELLS = 4096
 STEPS = 2
 
-VT, EN, VR, DE, VP = range(5)
-EARLY, LATE = (VT, EN, VR), (DE, VP)
+EN, VT, VR, DE, VP = range(5)
+EARLY, LATE = (EN, VT, VR), (DE, VP)
 GROUPS = (EARLY, LATE)
 SPANS = (pl.ds(0, 3), pl.ds(3, 2))
 S_VP = 3
@@ -67,9 +67,14 @@
     for k in range(1, AZ):
         pl.semaphore_signal(barrier, inc=1, device_id={"az": peers[k], "rad": rho}, device_id_type=MESH)
     cross = lax.rem(quad + 2 * half - 1 + QUADS, QUADS)
-    pl.semaphore_signal(
-        barrier, inc=1, device_id={"az": owner(pair, lax.rem(cross, 2)), "rad": lax.div(cross, 2)}, device_id_type=MESH
-    )
+    has_cross = jnp.logical_and(quad > 0, quad < QUADS - 1)
+
+    @pl.when(has_cross)
+    def _():
+        pl.semaphore_signal(
+            barrier, inc=1, device_id={"az": owner(pair, lax.rem(cross, 2)), "rad": lax.div(cross, 2)},
+            device_id_type=MESH,
+        )
 
     inner_t, inner_r = pl.ds(1, 2), pl.ds(1, 4)
     for buf, span in ((s0, pl.ds(0, 3)), (s1, pl.ds(0, 3)), (f0, pl.ds(0, 5)), (f1, pl.ds(0, 5))):
@@ -116,7 +121,7 @@
     for copy in loads:
         copy.wait()
     regroup(EARLY)
-    pl.semaphore_wait(barrier, AZ)
+    pl.semaphore_wait(barrier, AZ - 1 + has_cross.astype(jnp.int32))
     for k in ORDER:
         to_rows(k, 0).start()
     own_rows(0).start()
@@ -191,14 +196,16 @@
             ostage.at[SPANS[g], pl.ds(pl.multiple_of(a * 16, 16), 16), :], back.at[a, SPANS[g]], l_sem.at[2 + g]
         )
 
-    plans = [
-        (
-            halo(states[step], pl.ds(0, 2), pl.ds(1, 2), 3 * step),
-            halo(fresh[step], SPANS[1], SPANS[1], 3 * step + 1),
-            halo(fresh[step], SPANS[0], SPANS[0], 3 * step + 2),
-        )
-        for step in range(STEPS)
-    ]
+    plans = []
+    for step in range(STEPS):
+        s, f = states[step], fresh[step]
+        plans.append((
+            halo(s, EN, EN, 5 * step),
+            halo(s, VT, VR, 5 * step + 1),
+            halo(f, SPANS[1], SPANS[1], 5 * step + 2),
+            halo(f, EN, EN, 5 * step + 3),
+            halo(f, pl.ds(1, 2), pl.ds(1, 2), 5 * step + 4),
+        ))
 
     def along_azimuth(f, i, t, r, fields):
         p_lo = speed[i]
@@ -214,14 +221,15 @@
 
     for step in range(STEPS):
         s, f = states[step], fresh[step]
-        first, late, early = plans[step]
+        old_en, old_v, late, new_en, new_v = plans[step]
 
         if step == 0:
             for k in range(1, AZ):
                 to_rows(k, 0).wait_recv()
             own_rows(0).wait()
             unpack(EARLY)
-            each(first, "start")
+            each(old_v, "start")
+            each(old_en, "start")
             for k in range(1, AZ):
                 to_rows(k, 1).wait_recv()
             own_rows(1).wait()
@@ -245,13 +253,14 @@
             along_azimuth(f, i, t, r, LATE)
 
         eight(azimuth_late)
-        each(first, "wait_recv")
-
-        def source_rest(i, t, r):
+
+        def source_speeds(i, t, r):
             k = flux[VT, i]
-            e = s[EN, t, r]
             f[VR, t, r] = s[VR, t, r] - k * (s[EN, t, r + 1] - s[EN, t, r - 1])
             f[VT, t, r] = s[VT, t, r] - k * (s[EN, t + 1, r] - s[EN, t - 1, r])
+
+        def source_energy(i, t, r):
+            e = s[EN, t, r]
             div = (
                 flux[EN, i]
                 + (s[VR, t, r + 1] - s[VR, t, r - 1])
@@ -259,8 +268,11 @@
             )
             f[EN, t, r] = e - 0.01 * e * div
 
-        eight(source_rest, UNROLL)
-        each(early, "start")
+        turns = [(old_v, source_energy, new_en), (old_en, source_speeds, new_v)]
+        for needs, body, sends in turns if step == 0 else turns[::-1]:
+            each(needs, "wait_recv")
+            eight(body, UNROLL)
+            each(sends, "start")
 
         def azimuth_early(i, t, r):
             along_azimuth(f, i, t, r, EARLY)
@@ -289,10 +301,12 @@
         lax.fori_loop(0, 4, inner_theta, 0)
 
         each(late, "wait_recv")
-        each(early, "wait_recv")
-
-        for g in ((0, 1) if step < STEPS - 1 else (1, 0)):
-            fields = GROUPS[g]
+        each(new_v, "wait_recv")
+
+        last = step == STEPS - 1
+        for g, fields in ((1, LATE), (0, EARLY)) if last else ((0, (EN,)), (0, (VT, VR)), (1, LATE)):
+            if EN in fields:
+                each(new_en, "wait_recv")
 
             def outer_radius(t, _):
                 low = face(f, VR, (t + 1, 0), (t + 1, 1))
@@ -337,7 +351,7 @@
                             far = blended[q, i, pl.ds(lax.rem(whole + 8 * m + 1, CHUNKS), 8), :]
                             parts.append(pltpu.roll(jnp.where(lane8 < part, far, near), lax.rem(128 - part, 128), 1))
                         out = (1.0 - w) * parts[0] + w * parts[1]
-                        if step == STEPS - 1:
+                        if last:
                             ostage[q, pl.ds(64 * m + i, 8, stride=8), :] = out
                         elif q == DE:
                             f1[DE, t, r, pl.ds(8 * m, 8), :] = out
@@ -345,12 +359,14 @@
                             s1[S_VP if q == VP else q, t, r, pl.ds(8 * m, 8), :] = out
 
             eight(rotate, UNROLL)
-            if step == STEPS - 1:
+            if last:
                 for k in ORDER:
                     to_blocks(k, g).start()
                 own_blocks(g).start()
-            elif g == 0:
+            elif EN in fields:
                 each(plans[step + 1][0], "start")
+            elif VT in fields:
+                each(plans[step + 1][1], "start")
 
     for step in range(STEPS):
         for copies in plans[step]:
@@ -388,7 +404,7 @@
                         ]
             return 0
 
-        lax.fori_loop(0, 8, one, 0)
+        lax.fori_loop(0, 8, one, 0, unroll=8)
         writes.append(pltpu.make_async_copy(*targets[q], out_sem.at[q]))
         writes[-1].start()
     for copy in writes:
@@ -422,8 +438,8 @@
             pltpu.VMEM((5, 256, 128), f32),
             dma((2, AZ)),
             dma((2, AZ)),
-            dma((3 * STEPS, 4)),
-            dma((3 * STEPS, 4)),
+            dma((5 * STEPS, 4)),
+            dma((5 * STEPS, 4)),
             dma((2, AZ)),
             dma((2, AZ)),
             dma((4,)),

time: 50.2 us -> 47.4 us (0.944)
  the two profiles are of different devices: /device:TPU:1 before, /device:TPU:113 now
where the time goes in v2:
time: 47.4 us; the launch traced here: 47.3 us
  Pallas kernels  46.7 us (99%)
  between operations  0.64 us (1%)
    pallas_call x1, Pallas kernels, shards(): pl.pallas_call(kernel, out_shape=jax.ShapeDtypeStruct(block, f32), in_spe...  44.7 us
    pallas_call x1, Pallas kernels, shards(): pl.pallas_call(write_out, out_shape=tuple((jax.ShapeDtypeStruct(v.shape,...  1.94 us

profile of v2, /device:TPU:113, one launch (start us, length us, event | category | flops | bytes accessed | tf_op | source)
XLA Modules:
  0.0 47.3 jit_solution(8044532185929127630)
XLA Ops:
  0.6 44.7 %shard_map.76.back = f32[16,5,16,128]{3,2,1,0:T(8,128)} custom-call(f32[16,8,256]{2,1,0:T(8,128)} %den_hbm.1, f32[3,16,8,256]{3,2,1,0:T(8,128)} %vel_hbm.1, f32[16,8,256]{2,1,0:T(8,128)} %ene_hbm.1, s32[8]{0:T(128)} %shift_hbm.1, f32[8]{0:T(128)} %frac_hbm.1), custom_call_target="tpu_custom_call" | custom-call | tf_op jit(solution)/shard_map/pallas_call | solution.py:421
  45.4 1.9 %shard_map.77 = (f32[16,8,256]{2,1,0:T(8,128)}, f32[3,16,8,256]{3,2,1,0:T(8,128)}, f32[16,8,256]{2,1,0:T(8,128)}) custom-call(f32[16,5,16,128]{3,2,1,0:T(8,128)} %shard_map.76.back), custom_call_target="tpu_custom_call" | custom-call | tf_op jit(solution)/shard_map/pallas_call | solution.py:450

commit v3 on v2

--- a/solution.py
+++ b/solution.py
@@ -55,7 +55,7 @@
             (ene_hbm, ene_ref), (vel_hbm, vel_ref), (den_hbm, den_ref), (shift_hbm, shift_ref), (frac_hbm, frac_ref)
         ))
     ]
-    for copy in loads:
+    for copy in loads[:3]:
         copy.start()
 
     peers = []
@@ -75,6 +75,9 @@
             barrier, inc=1, device_id={"az": owner(pair, lax.rem(cross, 2)), "rad": lax.div(cross, 2)},
             device_id_type=MESH,
         )
+
+    for copy in loads[3:]:
+        copy.start()
 
     inner_t, inner_r = pl.ds(1, 2), pl.ds(1, 4)
     for buf, span in ((s0, pl.ds(0, 3)), (s1, pl.ds(0, 3)), (f0, pl.ds(0, 5)), (f1, pl.ds(0, 5))):
@@ -118,13 +121,15 @@
             stage.at[a, SPANS[g]], rows.at[SPANS[g], pl.ds(pl.multiple_of(a * 16, 16), 16), :], l_sem.at[g]
         )
 
-    for copy in loads:
+    for copy in loads[:2]:
         copy.wait()
     regroup(EARLY)
     pl.semaphore_wait(barrier, AZ - 1 + has_cross.astype(jnp.int32))
     for k in ORDER:
         to_rows(k, 0).start()
     own_rows(0).start()
+    for copy in loads[2:]:
+        copy.wait()
     regroup(LATE)
     for k in ORDER:
         to_rows(k, 1).start()
@@ -150,10 +155,10 @@
             )
 
         return (
+            (one(buf.at[r_fields, inner_t, 4], buf.at[r_fields, inner_t, 0], id_rup, 2), has_rup, has_rdn),
+            (one(buf.at[r_fields, inner_t, 1], buf.at[r_fields, inner_t, 5], id_rdn, 3), has_rdn, has_rup),
             (one(buf.at[t_fields, 2, inner_r], buf.at[t_fields, 0, inner_r], id_tup, 0), has_tup, has_tdn),
             (one(buf.at[t_fields, 1, inner_r], buf.at[t_fields, 3, inner_r], id_tdn, 1), has_tdn, has_tup),
-            (one(buf.at[r_fields, inner_t, 4], buf.at[r_fields, inner_t, 0], id_rup, 2), has_rup, has_rdn),
-            (one(buf.at[r_fields, inner_t, 1], buf.at[r_fields, inner_t, 5], id_rdn, 3), has_rdn, has_rup),
         )
 
     def each(copies, what):
@@ -200,11 +205,12 @@
     for step in range(STEPS):
         s, f = states[step], fresh[step]
         plans.append((
-            halo(s, EN, EN, 5 * step),
-            halo(s, VT, VR, 5 * step + 1),
-            halo(f, SPANS[1], SPANS[1], 5 * step + 2),
-            halo(f, EN, EN, 5 * step + 3),
-            halo(f, pl.ds(1, 2), pl.ds(1, 2), 5 * step + 4),
+            halo(s, EN, EN, 6 * step),
+            halo(s, VT, VR, 6 * step + 1),
+            halo(f, SPANS[1], SPANS[1], 6 * step + 2),
+            halo(f, EN, EN, 6 * step + 3),
+            halo(f, VT, VR, 6 * step + 4),
+            halo(f, VR, VT, 6 * step + 5),
         ))
 
     def along_azimuth(f, i, t, r, fields):
@@ -221,7 +227,7 @@
 
     for step in range(STEPS):
         s, f = states[step], fresh[step]
-        old_en, old_v, late, new_en, new_v = plans[step]
+        old_en, old_v, late, new_en, new_v, rest = plans[step]
 
         if step == 0:
             for k in range(1, AZ):
@@ -273,6 +279,7 @@
             each(needs, "wait_recv")
             eight(body, UNROLL)
             each(sends, "start")
+        each(rest, "start")
 
         def azimuth_early(i, t, r):
             along_azimuth(f, i, t, r, EARLY)
@@ -300,13 +307,16 @@
 
         lax.fori_loop(0, 4, inner_theta, 0)
 
-        each(late, "wait_recv")
         each(new_v, "wait_recv")
 
         last = step == STEPS - 1
         for g, fields in ((1, LATE), (0, EARLY)) if last else ((0, (EN,)), (0, (VT, VR)), (1, LATE)):
             if EN in fields:
                 each(new_en, "wait_recv")
+            if VT in fields:
+                each(rest, "wait_recv")
+            if DE in fields:
+                each(late, "wait_recv")
 
             def outer_radius(t, _):
                 low = face(f, VR, (t + 1, 0), (t + 1, 1))
@@ -332,7 +342,7 @@
                 for q in fields:
                     moved = f[q, t, r] - 0.025 * flux[q, i]
                     blended[q, i, pl.ds(0, CHUNKS), :] = moved
-                    blended[q, i, pl.ds(CHUNKS, 8), :] = moved[:8]
+                    blended[q, i, pl.ds(CHUNKS, CHUNKS), :] = moved
 
             eight(finish, UNROLL)
 
@@ -347,8 +357,8 @@
                     for m in range(4):
                         parts = []
                         for whole, part in views:
-                            near = blended[q, i, pl.ds(lax.rem(whole + 8 * m, CHUNKS), 8), :]
-                            far = blended[q, i, pl.ds(lax.rem(whole + 8 * m + 1, CHUNKS), 8), :]
+                            near = blended[q, i, pl.ds(whole + 8 * m, 8), :]
+                            far = blended[q, i, pl.ds(whole + 8 * m + 1, 8), :]
                             parts.append(pltpu.roll(jnp.where(lane8 < part, far, near), lax.rem(128 - part, 128), 1))
                         out = (1.0 - w) * parts[0] + w * parts[1]
                         if last:
@@ -434,12 +444,12 @@
             pltpu.VMEM((5, 4, 6, CHUNKS, 128), f32),
             pltpu.VMEM((8, CHUNKS, 128), f32),
             pltpu.VMEM((5, 8, CHUNKS, 128), f32),
-            pltpu.VMEM((5, 8, CHUNKS + 8, 128), f32),
+            pltpu.VMEM((5, 8, 2 * CHUNKS, 128), f32),
             pltpu.VMEM((5, 256, 128), f32),
             dma((2, AZ)),
             dma((2, AZ)),
-            dma((5 * STEPS, 4)),
-            dma((5 * STEPS, 4)),
+            dma((6 * STEPS, 4)),
+            dma((6 * STEPS, 4)),
             dma((2, AZ)),
             dma((2, AZ)),
             dma((4,)),

time: 47.4 us -> 45.5 us (0.960)
  Pallas kernels: 46.7 us -> 44.8 us
    pallas_call x1, Pallas kernels: 44.7 us -> 42.8 us  [shards(): pl.pallas_call(kernel, out_shape=jax.ShapeDtypeStruct(block, f32), in_spe...]
where the time goes in v3:
time: 45.5 us; the launch traced here: 45.4 us
  Pallas kernels  44.8 us (98%)
  between operations  0.64 us (1%)
    pallas_call x1, Pallas kernels, shards(): pl.pallas_call(kernel, out_shape=jax.ShapeDtypeStruct(block, f32), in_spe...  42.8 us
    pallas_call x1, Pallas kernels, shards(): pl.pallas_call(write_out, out_shape=tuple((jax.ShapeDtypeStruct(v.shape,...  1.94 us

profile of v3, /device:TPU:113, one launch (start us, length us, event | category | flops | bytes accessed | tf_op | source)
XLA Modules:
  0.0 45.4 jit_solution(3475125800127534790)
XLA Ops:
  0.6 42.8 %shard_map.76.back = f32[16,5,16,128]{3,2,1,0:T(8,128)} custom-call(f32[16,8,256]{2,1,0:T(8,128)} %den_hbm.1, f32[3,16,8,256]{3,2,1,0:T(8,128)} %vel_hbm.1, f32[16,8,256]{2,1,0:T(8,128)} %ene_hbm.1, s32[8]{0:T(128)} %shift_hbm.1, f32[8]{0:T(128)} %frac_hbm.1), custom_call_target="tpu_custom_call" | custom-call | tf_op jit(solution)/shard_map/pallas_call | solution.py:431
  43.5 1.9 %shard_map.77 = (f32[16,8,256]{2,1,0:T(8,128)}, f32[3,16,8,256]{3,2,1,0:T(8,128)}, f32[16,8,256]{2,1,0:T(8,128)}) custom-call(f32[16,5,16,128]{3,2,1,0:T(8,128)} %shard_map.76.back), custom_call_target="tpu_custom_call" | custom-call | tf_op jit(solution)/shard_map/pallas_call | solution.py:460

commit v4 on v3

--- a/solution.py
+++ b/solution.py
@@ -18,11 +18,11 @@
 SPANS = (pl.ds(0, 3), pl.ds(3, 2))
 S_VP = 3
 UNROLL = 8
-ORDER = (8, 4, 12, 2, 9, 5, 13, 3, 10, 6, 14, 1, 11, 7, 15)
+ORDER = (10, 8, 6, 4, 14, 12, 2, 11, 9, 7, 5, 15, 13, 3, 1)
 
 
 def owner(pair, half):
-    return lax.div(pair, 2) * 4 + half * 2 + lax.rem(pair, 2)
+    return lax.div(pair, 2) * 4 + (1 - half) * 2 + lax.rem(pair, 2)
 
 
 def prev_cell(x, lane):
@@ -44,7 +44,8 @@
 ):
     a = lax.axis_index("az")
     rho = lax.axis_index("rad")
-    x, half, core = lax.div(a, 4), lax.rem(lax.div(a, 2), 2), lax.rem(a, 2)
+    x, y, core = lax.div(a, 4), lax.rem(lax.div(a, 2), 2), lax.rem(a, 2)
+    half = 1 - y
     pair = 2 * x + core
     quad = 2 * rho + half
     states, fresh = (s0, s1), (f0, f1)
@@ -61,7 +62,7 @@
     peers = []
     for k in range(AZ):
         dx, dy, dc = k // 4, (k // 2) % 2, k % 2
-        peers.append(lax.rem(x + dx, 4) * 4 + lax.rem(half + dy, 2) * 2 + lax.rem(core + dc, 2))
+        peers.append(lax.rem(x + dx, 4) * 4 + lax.rem(y + dy, 2) * 2 + lax.rem(core + dc, 2))
 
     barrier = pltpu.get_barrier_semaphore()
     for k in range(1, AZ):

time: 45.5 us -> 43 us (0.945)
  the two profiles are of different devices: /device:TPU:113 before, /device:TPU:1 now
where the time goes in v4:
time: 43 us; the launch traced here: 42.9 us
  Pallas kernels  42.2 us (98%)
  between operations  0.64 us (1%)
    pallas_call x1, Pallas kernels, shards(): pl.pallas_call(kernel, out_shape=jax.ShapeDtypeStruct(block, f32), in_spe...  40.3 us
    pallas_call x1, Pallas kernels, shards(): pl.pallas_call(write_out, out_shape=tuple((jax.ShapeDtypeStruct(v.shape,...  1.94 us

profile of v4, /device:TPU:1, one launch (start us, length us, event | category | flops | bytes accessed | tf_op | source)
XLA Modules:
  0.0 42.9 jit_solution(12528003906051408475)
XLA Ops:
  0.6 40.3 %shard_map.76.back = f32[16,5,16,128]{3,2,1,0:T(8,128)} custom-call(f32[16,8,256]{2,1,0:T(8,128)} %den_hbm.1, f32[3,16,8,256]{3,2,1,0:T(8,128)} %vel_hbm.1, f32[16,8,256]{2,1,0:T(8,128)} %ene_hbm.1, s32[8]{0:T(128)} %shift_hbm.1, f32[8]{0:T(128)} %frac_hbm.1), custom_call_target="tpu_custom_call" | custom-call | tf_op jit(solution)/shard_map/pallas_call | solution.py:432
  40.9 1.9 %shard_map.77 = (f32[16,8,256]{2,1,0:T(8,128)}, f32[3,16,8,256]{3,2,1,0:T(8,128)}, f32[16,8,256]{2,1,0:T(8,128)}) custom-call(f32[16,5,16,128]{3,2,1,0:T(8,128)} %shard_map.76.back), custom_call_target="tpu_custom_call" | custom-call | tf_op jit(solution)/shard_map/pallas_call | solution.py:461

commit v5 on v4

--- a/solution.py
+++ b/solution.py
@@ -16,7 +16,8 @@
 EARLY, LATE = (EN, VT, VR), (DE, VP)
 GROUPS = (EARLY, LATE)
 SPANS = (pl.ds(0, 3), pl.ds(3, 2))
-S_VP = 3
+S_AT = {VR: 0, EN: 1, VT: 2, VP: 3}
+F_AT = {DE: 0, VP: 1, VR: 2, EN: 3, VT: 4}
 UNROLL = 8
 ORDER = (10, 8, 6, 4, 14, 12, 2, 11, 9, 7, 5, 15, 13, 3, 1)
 
@@ -39,7 +40,7 @@
     den_hbm, vel_hbm, ene_hbm, shift_hbm, frac_hbm,
     back,
     den_ref, vel_ref, ene_ref, shift_ref, frac_ref,
-    stage, rows, s0, s1, f0, f1, speed, flux, blended, ostage,
+    stage, rows, s0, s1, f0, f1, speed, factor, along, flux, blended, ostage,
     a_send, a_recv, h_send, h_recv, b_send, b_recv, l_sem, i_sem,
 ):
     a = lax.axis_index("az")
@@ -112,14 +113,14 @@
             src_ref=stage.at[dest, SPANS[g]],
             dst_ref=rows.at[SPANS[g], pl.ds(pl.multiple_of(a * 16, 16), 16), :],
             send_sem=a_send.at[g, k],
-            recv_sem=a_recv.at[g, k],
+            recv_sem=a_recv.at[g],
             device_id={"az": dest, "rad": rho},
             device_id_type=MESH,
         )
 
     def own_rows(g):
         return pltpu.make_async_copy(
-            stage.at[a, SPANS[g]], rows.at[SPANS[g], pl.ds(pl.multiple_of(a * 16, 16), 16), :], l_sem.at[g]
+            stage.at[a, SPANS[g]], rows.at[SPANS[g], pl.ds(pl.multiple_of(a * 16, 16), 16), :], a_recv.at[g]
         )
 
     for copy in loads[:2]:
@@ -180,9 +181,9 @@
             for q in fields:
                 value = rows[q, pl.ds(i, CHUNKS, stride=8), :]
                 if q == DE:
-                    f0[DE, t, r] = value
+                    f0[F_AT[DE], t, r] = value
                 else:
-                    s0[S_VP if q == VP else q, t, r] = value
+                    s0[S_AT[q], t, r] = value
 
         eight(one)
 
@@ -192,69 +193,72 @@
             src_ref=ostage.at[SPANS[g], pl.ds(pl.multiple_of(dest * 16, 16), 16), :],
             dst_ref=back.at[a, SPANS[g]],
             send_sem=b_send.at[g, k],
-            recv_sem=b_recv.at[g, k],
+            recv_sem=b_recv.at[g],
             device_id={"az": dest, "rad": rho},
             device_id_type=MESH,
         )
 
     def own_blocks(g):
         return pltpu.make_async_copy(
-            ostage.at[SPANS[g], pl.ds(pl.multiple_of(a * 16, 16), 16), :], back.at[a, SPANS[g]], l_sem.at[2 + g]
-        )
-
-    plans = []
-    for step in range(STEPS):
-        s, f = states[step], fresh[step]
-        plans.append((
-            halo(s, EN, EN, 6 * step),
-            halo(s, VT, VR, 6 * step + 1),
-            halo(f, SPANS[1], SPANS[1], 6 * step + 2),
-            halo(f, EN, EN, 6 * step + 3),
-            halo(f, VT, VR, 6 * step + 4),
-            halo(f, VR, VT, 6 * step + 5),
-        ))
+            ostage.at[SPANS[g], pl.ds(pl.multiple_of(a * 16, 16), 16), :], back.at[a, SPANS[g]], b_recv.at[g]
+        )
+
+    def old_halo(step, slot):
+        return halo(states[step], S_AT[EN], S_AT[EN], slot), halo(states[step], S_AT[VT], S_AT[VR], slot + 1)
+
+    def new_halo(step, slot):
+        f = fresh[step]
+        return halo(f, pl.ds(0, 2), pl.ds(0, 2), slot), halo(f, F_AT[VT], F_AT[VR], slot + 1)
+
+    old_both = halo(s0, pl.ds(1, 2), pl.ds(0, 2), 0)
+    new_en, rest = halo(f0, F_AT[EN], F_AT[EN], 1), halo(f0, F_AT[VR], F_AT[VT], 2)
+    late0, new_v0 = new_halo(0, 3)
+    old_en, old_v = old_halo(1, 5)
+    late1, new_v1 = new_halo(1, 7)
+    new_both = halo(f1, pl.ds(2, 2), pl.ds(3, 2), 9)
+    lates, news = (late0, late1), (new_v0, new_v1)
+    halos = (old_both, new_en, rest, late0, new_v0, old_en, old_v, late1, new_v1, new_both)
 
     def along_azimuth(f, i, t, r, fields):
         p_lo = speed[i]
         for q in fields:
-            v = f[q, t, r]
+            v = f[F_AT[q], t, r]
             low = p_lo * jnp.where(p_lo > 0, prev_cell(v, lane), v)
             flux[q, i] = next_cell(low, lane) - low
 
     def face(f, u, below, above):
-        s = f[(u,) + below] + f[(u,) + above]
+        s = f[(F_AT[u],) + below] + f[(F_AT[u],) + above]
         up = s > 0
-        return lambda q: s * jnp.where(up, f[(q,) + below], f[(q,) + above])
+        return lambda q: s * jnp.where(up, f[(F_AT[q],) + below], f[(F_AT[q],) + above])
+
+    def begin(step):
+        s, f = states[step], fresh[step]
+
+        def source_azimuth(i, t, r):
+            den = f[F_AT[DE], t, r]
+            k = 0.01 / jnp.where(den > 0, den, 1.0)
+            e = s[S_AT[EN], t, r]
+            vp = s[S_AT[VP], t, r]
+            new = vp - k * (next_cell(e, lane) - prev_cell(e, lane))
+            f[F_AT[VP], t, r] = new
+            factor[i] = k
+            along[i] = next_cell(vp, lane) - prev_cell(vp, lane)
+            speed[i] = new + prev_cell(new, lane)
+
+        eight(source_azimuth, UNROLL)
+        each(lates[step], "start")
 
     for step in range(STEPS):
         s, f = states[step], fresh[step]
-        old_en, old_v, late, new_en, new_v, rest = plans[step]
+        last = step == STEPS - 1
 
         if step == 0:
-            for k in range(1, AZ):
-                to_rows(k, 0).wait_recv()
-            own_rows(0).wait()
+            pltpu.make_async_copy(rows.at[SPANS[0]], rows.at[SPANS[0]], a_recv.at[0]).wait()
             unpack(EARLY)
-            each(old_v, "start")
-            each(old_en, "start")
-            for k in range(1, AZ):
-                to_rows(k, 1).wait_recv()
-            own_rows(1).wait()
+            each(old_both, "start")
+            pltpu.make_async_copy(rows.at[SPANS[1]], rows.at[SPANS[1]], a_recv.at[1]).wait()
             unpack(LATE)
-
-        def source_azimuth(i, t, r):
-            den = f[DE, t, r]
-            k = 0.01 / jnp.where(den > 0, den, 1.0)
-            e = s[EN, t, r]
-            vp = s[S_VP, t, r]
-            new = vp - k * (next_cell(e, lane) - prev_cell(e, lane))
-            f[VP, t, r] = new
-            flux[VT, i] = k
-            flux[EN, i] = next_cell(vp, lane) - prev_cell(vp, lane)
-            speed[i] = new + prev_cell(new, lane)
-
-        eight(source_azimuth, UNROLL)
-        each(late, "start")
+            begin(0)
 
         def azimuth_late(i, t, r):
             along_azimuth(f, i, t, r, LATE)
@@ -262,25 +266,33 @@
         eight(azimuth_late)
 
         def source_speeds(i, t, r):
-            k = flux[VT, i]
-            f[VR, t, r] = s[VR, t, r] - k * (s[EN, t, r + 1] - s[EN, t, r - 1])
-            f[VT, t, r] = s[VT, t, r] - k * (s[EN, t + 1, r] - s[EN, t - 1, r])
+            k = factor[i]
+            f[F_AT[VR], t, r] = s[S_AT[VR], t, r] - k * (s[S_AT[EN], t, r + 1] - s[S_AT[EN], t, r - 1])
+            f[F_AT[VT], t, r] = s[S_AT[VT], t, r] - k * (s[S_AT[EN], t + 1, r] - s[S_AT[EN], t - 1, r])
 
         def source_energy(i, t, r):
-            e = s[EN, t, r]
+            e = s[S_AT[EN], t, r]
             div = (
-                flux[EN, i]
-                + (s[VR, t, r + 1] - s[VR, t, r - 1])
-                + (s[VT, t + 1, r] - s[VT, t - 1, r])
+                along[i]
+                + (s[S_AT[VR], t, r + 1] - s[S_AT[VR], t, r - 1])
+                + (s[S_AT[VT], t + 1, r] - s[S_AT[VT], t - 1, r])
             )
-            f[EN, t, r] = e - 0.01 * e * div
-
-        turns = [(old_v, source_energy, new_en), (old_en, source_speeds, new_v)]
-        for needs, body, sends in turns if step == 0 else turns[::-1]:
-            each(needs, "wait_recv")
-            eight(body, UNROLL)
-            each(sends, "start")
-        each(rest, "start")
+            f[F_AT[EN], t, r] = e - 0.01 * e * div
+
+        if last:
+            each(old_en, "wait_recv")
+            eight(source_speeds, UNROLL)
+            each(new_v1, "start")
+            each(old_v, "wait_recv")
+            eight(source_energy, UNROLL)
+            each(new_both, "start")
+        else:
+            each(old_both, "wait_recv")
+            eight(source_energy, UNROLL)
+            each(new_en, "start")
+            eight(source_speeds, UNROLL)
+            each(new_v0, "start")
+            each(rest, "start")
 
         def azimuth_early(i, t, r):
             along_azimuth(f, i, t, r, EARLY)
@@ -308,16 +320,15 @@
 
         lax.fori_loop(0, 4, inner_theta, 0)
 
-        each(new_v, "wait_recv")
-
-        last = step == STEPS - 1
+        each(news[step], "wait_recv")
+
         for g, fields in ((1, LATE), (0, EARLY)) if last else ((0, (EN,)), (0, (VT, VR)), (1, LATE)):
-            if EN in fields:
-                each(new_en, "wait_recv")
-            if VT in fields:
-                each(rest, "wait_recv")
             if DE in fields:
-                each(late, "wait_recv")
+                each(lates[step], "wait_recv")
+            elif last:
+                each(new_both, "wait_recv")
+            else:
+                each(new_en if EN in fields else rest, "wait_recv")
 
             def outer_radius(t, _):
                 low = face(f, VR, (t + 1, 0), (t + 1, 1))
@@ -341,7 +352,7 @@
 
             def finish(i, t, r):
                 for q in fields:
-                    moved = f[q, t, r] - 0.025 * flux[q, i]
+                    moved = f[F_AT[q], t, r] - 0.025 * flux[q, i]
                     blended[q, i, pl.ds(0, CHUNKS), :] = moved
                     blended[q, i, pl.ds(CHUNKS, CHUNKS), :] = moved
 
@@ -365,9 +376,9 @@
                         if last:
                             ostage[q, pl.ds(64 * m + i, 8, stride=8), :] = out
                         elif q == DE:
-                            f1[DE, t, r, pl.ds(8 * m, 8), :] = out
+                            f1[F_AT[DE], t, r, pl.ds(8 * m, 8), :] = out
                         else:
-                            s1[S_VP if q == VP else q, t, r, pl.ds(8 * m, 8), :] = out
+                            s1[S_AT[q], t, r, pl.ds(8 * m, 8), :] = out
 
             eight(rotate, UNROLL)
             if last:
@@ -375,21 +386,20 @@
                     to_blocks(k, g).start()
                 own_blocks(g).start()
             elif EN in fields:
-                each(plans[step + 1][0], "start")
+                each(old_en, "start")
             elif VT in fields:
-                each(plans[step + 1][1], "start")
-
-    for step in range(STEPS):
-        for copies in plans[step]:
-            each(copies, "wait_send")
+                each(old_v, "start")
+            else:
+                begin(step + 1)
+
+    for copies in halos:
+        each(copies, "wait_send")
     for g in range(2):
         for k in range(1, AZ):
             to_rows(k, g).wait_send()
             to_blocks(k, g).wait_send()
     for g in range(2):
-        own_blocks(g).wait()
-        for k in range(1, AZ):
-            to_blocks(k, g).wait_recv()
+        pltpu.make_async_copy(back.at[:, SPANS[g]], back.at[:, SPANS[g]], b_recv.at[g]).wait()
 
 
 def write_out(back, den_hbm, vel_hbm, ene_hbm, blocks, den_out, vel_out, ene_out, in_sem, out_sem):
@@ -444,15 +454,17 @@
             pltpu.VMEM((5, 4, 6, CHUNKS, 128), f32),
             pltpu.VMEM((5, 4, 6, CHUNKS, 128), f32),
             pltpu.VMEM((8, CHUNKS, 128), f32),
+            pltpu.VMEM((8, CHUNKS, 128), f32),
+            pltpu.VMEM((8, CHUNKS, 128), f32),
             pltpu.VMEM((5, 8, CHUNKS, 128), f32),
             pltpu.VMEM((5, 8, 2 * CHUNKS, 128), f32),
             pltpu.VMEM((5, 256, 128), f32),
             dma((2, AZ)),
+            dma((2,)),
+            dma((10, 4)),
+            dma((10, 4)),
             dma((2, AZ)),
-            dma((6 * STEPS, 4)),
-            dma((6 * STEPS, 4)),
-            dma((2, AZ)),
-            dma((2, AZ)),
+            dma((2,)),
             dma((4,)),
             dma((5,)),
         ],

time: 43 us -> 42.3 us (0.984)
  Pallas kernels: 42.2 us -> 41.5 us
    pallas_call x1, Pallas kernels: 40.3 us -> 39.6 us  [shards(): pl.pallas_call(kernel, out_shape=jax.ShapeDtypeStruct(block, f32), in_spe...]
where the time goes in v5:
time: 42.3 us; the launch traced here: 42.1 us
  Pallas kernels  41.5 us (98%)
  between operations  0.64 us (2%)
    pallas_call x1, Pallas kernels, shards(): pl.pallas_call(kernel, out_shape=jax.ShapeDtypeStruct(block, f32), in_spe...  39.6 us
    pallas_call x1, Pallas kernels, shards(): pl.pallas_call(write_out, out_shape=tuple((jax.ShapeDtypeStruct(v.shape,...  1.94 us

profile of v5, /device:TPU:1, one launch (start us, length us, event | category | flops | bytes accessed | tf_op | source)
XLA Modules:
  0.0 42.1 jit_solution(5514064115050210653)
XLA Ops:
  0.6 39.6 %shard_map.76.back = f32[16,5,16,128]{3,2,1,0:T(8,128)} custom-call(f32[16,8,256]{2,1,0:T(8,128)} %den_hbm.1, f32[3,16,8,256]{3,2,1,0:T(8,128)} %vel_hbm.1, f32[16,8,256]{2,1,0:T(8,128)} %ene_hbm.1, s32[8]{0:T(128)} %shift_hbm.1, f32[8]{0:T(128)} %frac_hbm.1), custom_call_target="tpu_custom_call" | custom-call | tf_op jit(solution)/shard_map/pallas_call | solution.py:442
  40.2 1.9 %shard_map.77 = (f32[16,8,256]{2,1,0:T(8,128)}, f32[3,16,8,256]{3,2,1,0:T(8,128)}, f32[16,8,256]{2,1,0:T(8,128)}) custom-call(f32[16,5,16,128]{3,2,1,0:T(8,128)} %shard_map.76.back), custom_call_target="tpu_custom_call" | custom-call | tf_op jit(solution)/shard_map/pallas_call | solution.py:473

commit v6 on v5

--- a/solution.py
+++ b/solution.py
@@ -402,17 +402,13 @@
         pltpu.make_async_copy(back.at[:, SPANS[g]], back.at[:, SPANS[g]], b_recv.at[g]).wait()
 
 
-def write_out(back, den_hbm, vel_hbm, ene_hbm, blocks, den_out, vel_out, ene_out, in_sem, out_sem):
+def write_out(back, den_hbm, vel_hbm, ene_hbm, den_out, vel_out, ene_out, out_sem):
     targets = {
         VT: (vel_out.at[2], vel_hbm.at[2]), EN: (ene_out, ene_hbm), VR: (vel_out.at[1], vel_hbm.at[1]),
         DE: (den_out, den_hbm), VP: (vel_out.at[0], vel_hbm.at[0]),
     }
-    reads = [pltpu.make_async_copy(back.at[:, q], blocks.at[:, q], in_sem.at[q]) for q in range(5)]
-    for copy in reads:
-        copy.start()
     writes = []
     for q in range(5):
-        reads[q].wait()
         dst = targets[q][0]
 
         def one(tp, _):
@@ -420,7 +416,7 @@
                 src = owner(tp, h)
                 for c in range(2):
                     for t in range(2):
-                        dst[2 * tp + t, pl.ds(4 * h, 4), pl.ds(128 * c, 128)] = blocks[
+                        dst[2 * tp + t, pl.ds(4 * h, 4), pl.ds(128 * c, 128)] = back[
                             src, q, pl.ds(c * 8 + t * 4, 4), :
                         ]
             return 0
@@ -435,13 +431,13 @@
 def shards(density, velocity, energy, shifts, fraction):
     hbm = pl.BlockSpec(memory_space=pl.ANY)
     f32 = jnp.float32
-    limit = 60 * 1024 * 1024
+    limit = 40 * 1024 * 1024
     block = (AZ, 5, 16, 128)
     dma = pltpu.SemaphoreType.DMA
     fields = [pltpu.VMEM(v.shape, f32) for v in (density, velocity, energy)]
     back = pl.pallas_call(
         kernel,
-        out_shape=jax.ShapeDtypeStruct(block, f32),
+        out_shape=pltpu.VMEM(block, f32),
         in_specs=[hbm] * 5,
         out_specs=hbm,
         scratch_shapes=fields + [
@@ -469,15 +465,15 @@
             dma((5,)),
         ],
         compiler_params=pltpu.CompilerParams(collective_id=0, has_side_effects=True, vmem_limit_bytes=limit),
-    )(density, velocity, energy, shifts, fraction)
+    )(*(pltpu.with_memory_space_constraint(v, pltpu.HBM) for v in (density, velocity, energy, shifts, fraction)))
     return pl.pallas_call(
         write_out,
         out_shape=tuple(jax.ShapeDtypeStruct(v.shape, f32) for v in (density, velocity, energy)),
-        in_specs=[hbm],
+        in_specs=[pl.BlockSpec(memory_space=pltpu.VMEM)],
         out_specs=(hbm,) * 3,
-        scratch_shapes=[pltpu.VMEM(block, f32)] + fields + [dma((5,)), dma((5,))],
-        compiler_params=pltpu.CompilerParams(vmem_limit_bytes=limit),
-    )(back)
+        scratch_shapes=fields + [dma((5,))],
+        compiler_params=pltpu.CompilerParams(vmem_limit_bytes=16 * 1024 * 1024),
+    )(pltpu.with_memory_space_constraint(back, pltpu.VMEM))
 
 
 def solution(mesh):

time: 42.3 us -> 41.1 us (0.972)
  Pallas kernels: 41.5 us -> 40.3 us
    pallas_call x1, Pallas kernels: 1.94 us -> 0.9 us  [shards(): pl.pallas_call(write_out, out_shape=tuple((jax.ShapeDtypeStruct(v.shape,...]
where the time goes in v6:
time: 41.1 us; the launch traced here: 41 us
  Pallas kernels  40.3 us (98%)
  between operations  0.64 us (2%)
    pallas_call x1, Pallas kernels, shards(): pl.pallas_call(kernel, out_shape=pltpu.VMEM(block, f32), in_specs=[hbm] *...  39.4 us
    pallas_call x1, Pallas kernels, shards(): pl.pallas_call(write_out, out_shape=tuple((jax.ShapeDtypeStruct(v.shape,...  0.9 us

profile of v6, /device:TPU:1, one launch (start us, length us, event | category | flops | bytes accessed | tf_op | source)
XLA Modules:
  0.0 41.0 jit_solution(4290646310823252147)
XLA Ops:
  0.6 39.4 %shard_map.76.back = f32[16,5,16,128]{3,2,1,0:T(8,128)S(1)} custom-call(f32[16,8,256]{2,1,0:T(8,128)} %den_hbm.1, f32[3,16,8,256]{3,2,1,0:T(8,128)} %vel_hbm.1, f32[16,8,256]{2,1,0:T(8,128)} %ene_hbm.1, s32[8]{0:T(128)} %shift_hbm.1, f32[8]{0:T(128)} %frac_hbm.1), custom_call_target="tpu_custom_call" | custom-call | tf_op jit(solution)/shard_map/pallas_call | solution.py:438
  40.1 0.9 %shard_map.77 = (f32[16,8,256]{2,1,0:T(8,128)}, f32[3,16,8,256]{3,2,1,0:T(8,128)}, f32[16,8,256]{2,1,0:T(8,128)}) custom-call(f32[16,5,16,128]{3,2,1,0:T(8,128)S(1)} %shard_map.76.back), custom_call_target="tpu_custom_call" | custom-call | tf_op jit(solution)/shard_map/pallas_call | solution.py:469

commit v7 on v6

--- a/solution.py
+++ b/solution.py
@@ -82,14 +82,22 @@
         copy.start()
 
     inner_t, inner_r = pl.ds(1, 2), pl.ds(1, 4)
-    for buf, span in ((s0, pl.ds(0, 3)), (s1, pl.ds(0, 3)), (f0, pl.ds(0, 5)), (f1, pl.ds(0, 5))):
-        def clear(where):
-            buf[where] = jnp.zeros_like(buf[where])
-
-        pl.when(pair == 0)(lambda: clear((span, 0, inner_r)))
-        pl.when(pair == 7)(lambda: clear((span, 3, inner_r)))
-        pl.when(quad == 0)(lambda: clear((span, inner_t, 0)))
-        pl.when(quad == QUADS - 1)(lambda: clear((span, inner_t, 5)))
+    own_t, own_r = pl.ds(2, 2), pl.ds(2, 4)
+    low_two = pl.ds(0, 2)
+
+    def clear(buf, where):
+        buf[where] = jnp.zeros_like(buf[where])
+
+    for buf in (f0, f1):
+        pl.when(pair == 0)(lambda: clear(buf, (pl.ds(0, 5), 0, inner_r)))
+        pl.when(pair == 7)(lambda: clear(buf, (pl.ds(0, 5), 3, inner_r)))
+        pl.when(quad == 0)(lambda: clear(buf, (pl.ds(0, 5), inner_t, 0)))
+        pl.when(quad == QUADS - 1)(lambda: clear(buf, (pl.ds(0, 5), inner_t, 5)))
+    for buf in (s0, s1):
+        pl.when(pair == 0)(lambda: clear(buf, (pl.ds(0, 3), low_two, own_r)))
+        pl.when(pair == 7)(lambda: clear(buf, (pl.ds(0, 3), pl.ds(4, 2), own_r)))
+        pl.when(quad == 0)(lambda: clear(buf, (pl.ds(0, 3), own_t, low_two)))
+        pl.when(quad == QUADS - 1)(lambda: clear(buf, (pl.ds(0, 3), own_t, pl.ds(6, 2))))
 
     sources = {VT: vel_ref.at[2], EN: ene_ref, VR: vel_ref.at[1], DE: den_ref, VP: vel_ref.at[0]}
 
@@ -149,18 +157,47 @@
     id_rup = {"az": owner(pair, lax.rem(r_up, 2)), "rad": lax.div(r_up, 2)}
     id_rdn = {"az": owner(pair, lax.rem(r_dn, 2)), "rad": lax.div(r_dn, 2)}
 
+    def four(slot, r_up, r_dn, t_up, t_dn):
+        def one(pair_of_refs, ident, d):
+            return pltpu.make_async_remote_copy(
+                src_ref=pair_of_refs[0], dst_ref=pair_of_refs[1], send_sem=h_send.at[slot, d],
+                recv_sem=h_recv.at[slot, d], device_id=ident, device_id_type=MESH,
+            )
+
+        return (
+            (one(r_up, id_rup, 2), has_rup, has_rdn),
+            (one(r_dn, id_rdn, 3), has_rdn, has_rup),
+            (one(t_up, id_tup, 0), has_tup, has_tdn),
+            (one(t_dn, id_tdn, 1), has_tdn, has_tup),
+        )
+
+    def old_energy(step, slot):
+        en = states[step].at[S_AT[EN]]
+        return four(
+            slot,
+            (en.at[own_t, pl.ds(4, 2)], en.at[own_t, low_two]),
+            (en.at[own_t, pl.ds(2, 2)], en.at[own_t, pl.ds(6, 2)]),
+            (en.at[own_t, own_r], en.at[low_two, own_r]),
+            (en.at[own_t, own_r], en.at[pl.ds(4, 2), own_r]),
+        )
+
+    def old_speeds(step, slot):
+        vt, vr = states[step].at[S_AT[VT]], states[step].at[S_AT[VR]]
+        return four(
+            slot,
+            (vr.at[own_t, 5], vr.at[own_t, 1]),
+            (vr.at[own_t, 2], vr.at[own_t, 6]),
+            (vt.at[3, own_r], vt.at[1, own_r]),
+            (vt.at[2, own_r], vt.at[4, own_r]),
+        )
+
     def halo(buf, t_fields, r_fields, slot):
-        def one(src, dst, ident, d):
-            return pltpu.make_async_remote_copy(
-                src_ref=src, dst_ref=dst, send_sem=h_send.at[slot, d], recv_sem=h_recv.at[slot, d],
-                device_id=ident, device_id_type=MESH,
-            )
-
-        return (
-            (one(buf.at[r_fields, inner_t, 4], buf.at[r_fields, inner_t, 0], id_rup, 2), has_rup, has_rdn),
-            (one(buf.at[r_fields, inner_t, 1], buf.at[r_fields, inner_t, 5], id_rdn, 3), has_rdn, has_rup),
-            (one(buf.at[t_fields, 2, inner_r], buf.at[t_fields, 0, inner_r], id_tup, 0), has_tup, has_tdn),
-            (one(buf.at[t_fields, 1, inner_r], buf.at[t_fields, 3, inner_r], id_tdn, 1), has_tdn, has_tup),
+        return four(
+            slot,
+            (buf.at[r_fields, inner_t, 4], buf.at[r_fields, inner_t, 0]),
+            (buf.at[r_fields, inner_t, 1], buf.at[r_fields, inner_t, 5]),
+            (buf.at[t_fields, 2, inner_r], buf.at[t_fields, 0, inner_r]),
+            (buf.at[t_fields, 1, inner_r], buf.at[t_fields, 3, inner_r]),
         )
 
     def each(copies, what):
@@ -183,7 +220,7 @@
                 if q == DE:
                     f0[F_AT[DE], t, r] = value
                 else:
-                    s0[S_AT[q], t, r] = value
+                    s0[S_AT[q], t + 1, r + 1] = value
 
         eight(one)
 
@@ -203,21 +240,12 @@
             ostage.at[SPANS[g], pl.ds(pl.multiple_of(a * 16, 16), 16), :], back.at[a, SPANS[g]], b_recv.at[g]
         )
 
-    def old_halo(step, slot):
-        return halo(states[step], S_AT[EN], S_AT[EN], slot), halo(states[step], S_AT[VT], S_AT[VR], slot + 1)
-
-    def new_halo(step, slot):
-        f = fresh[step]
-        return halo(f, pl.ds(0, 2), pl.ds(0, 2), slot), halo(f, F_AT[VT], F_AT[VR], slot + 1)
-
-    old_both = halo(s0, pl.ds(1, 2), pl.ds(0, 2), 0)
-    new_en, rest = halo(f0, F_AT[EN], F_AT[EN], 1), halo(f0, F_AT[VR], F_AT[VT], 2)
-    late0, new_v0 = new_halo(0, 3)
-    old_en, old_v = old_halo(1, 5)
-    late1, new_v1 = new_halo(1, 7)
-    new_both = halo(f1, pl.ds(2, 2), pl.ds(3, 2), 9)
-    lates, news = (late0, late1), (new_v0, new_v1)
-    halos = (old_both, new_en, rest, late0, new_v0, old_en, old_v, late1, new_v1, new_both)
+    olds_en = (old_energy(0, 0), old_energy(1, 1))
+    olds_v = (old_speeds(0, 2), old_speeds(1, 3))
+    lates = tuple(halo(fresh[step], pl.ds(0, 2), pl.ds(0, 2), 4 + step) for step in range(STEPS))
+    new_ens = tuple(halo(fresh[step], F_AT[EN], F_AT[EN], 6 + step) for step in range(STEPS))
+    rests = tuple(halo(fresh[step], F_AT[VR], F_AT[VT], 8 + step) for step in range(STEPS))
+    halos = olds_en + olds_v + lates + new_ens + rests
 
     def along_azimuth(f, i, t, r, fields):
         p_lo = speed[i]
@@ -237,8 +265,8 @@
         def source_azimuth(i, t, r):
             den = f[F_AT[DE], t, r]
             k = 0.01 / jnp.where(den > 0, den, 1.0)
-            e = s[S_AT[EN], t, r]
-            vp = s[S_AT[VP], t, r]
+            e = s[S_AT[EN], t + 1, r + 1]
+            vp = s[S_AT[VP], t + 1, r + 1]
             new = vp - k * (next_cell(e, lane) - prev_cell(e, lane))
             f[F_AT[VP], t, r] = new
             factor[i] = k
@@ -255,7 +283,8 @@
         if step == 0:
             pltpu.make_async_copy(rows.at[SPANS[0]], rows.at[SPANS[0]], a_recv.at[0]).wait()
             unpack(EARLY)
-            each(old_both, "start")
+            each(olds_en[0], "start")
+            each(olds_v[0], "start")
             pltpu.make_async_copy(rows.at[SPANS[1]], rows.at[SPANS[1]], a_recv.at[1]).wait()
             unpack(LATE)
             begin(0)
@@ -267,68 +296,106 @@
 
         def source_speeds(i, t, r):
             k = factor[i]
-            f[F_AT[VR], t, r] = s[S_AT[VR], t, r] - k * (s[S_AT[EN], t, r + 1] - s[S_AT[EN], t, r - 1])
-            f[F_AT[VT], t, r] = s[S_AT[VT], t, r] - k * (s[S_AT[EN], t + 1, r] - s[S_AT[EN], t - 1, r])
+            f[F_AT[VR], t, r] = s[S_AT[VR], t + 1, r + 1] - k * (s[S_AT[EN], t + 1, r + 2] - s[S_AT[EN], t + 1, r])
+            f[F_AT[VT], t, r] = s[S_AT[VT], t + 1, r + 1] - k * (s[S_AT[EN], t + 2, r + 1] - s[S_AT[EN], t, r + 1])
 
         def source_energy(i, t, r):
-            e = s[S_AT[EN], t, r]
+            e = s[S_AT[EN], t + 1, r + 1]
             div = (
                 along[i]
-                + (s[S_AT[VR], t, r + 1] - s[S_AT[VR], t, r - 1])
-                + (s[S_AT[VT], t + 1, r] - s[S_AT[VT], t - 1, r])
+                + (s[S_AT[VR], t + 1, r + 2] - s[S_AT[VR], t + 1, r])
+                + (s[S_AT[VT], t + 2, r + 1] - s[S_AT[VT], t, r + 1])
             )
             f[F_AT[EN], t, r] = e - 0.01 * e * div
 
+        def beyond(u, place, near, far, own):
+            den = f[(F_AT[DE],) + place]
+            k = 0.01 / jnp.where(den > 0, den, 1.0)
+            low, high = (far, own) if near < own else (own, far)
+            en = S_AT[EN]
+            t, r = place
+            if u == VT:
+                new = s[S_AT[VT], near, r + 1] - k * (s[en, high, r + 1] - s[en, low, r + 1])
+            else:
+                new = s[S_AT[VR], t + 1, near] - k * (s[en, t + 1, high] - s[en, t + 1, low])
+            f[(F_AT[u],) + place] = new
+
+        def all_beyond():
+            @pl.when(has_tdn)
+            def _():
+                for r in range(1, 5):
+                    beyond(VT, (0, r), 1, 0, 2)
+
+            @pl.when(has_tup)
+            def _():
+                for r in range(1, 5):
+                    beyond(VT, (3, r), 4, 5, 3)
+
+            @pl.when(has_rdn)
+            def _():
+                for t in range(1, 3):
+                    beyond(VR, (t, 0), 1, 0, 2)
+
+            @pl.when(has_rup)
+            def _():
+                for t in range(1, 3):
+                    beyond(VR, (t, 5), 6, 7, 5)
+
         if last:
-            each(old_en, "wait_recv")
+            each(olds_v[1], "wait_recv")
+            eight(source_energy, UNROLL)
+            each(new_ens[1], "start")
+            each(olds_en[1], "wait_recv")
             eight(source_speeds, UNROLL)
-            each(new_v1, "start")
-            each(old_v, "wait_recv")
+            each(rests[1], "start")
+        else:
+            each(olds_en[0], "wait_recv")
+            eight(source_speeds, UNROLL)
+            each(rests[0], "start")
+            each(olds_v[0], "wait_recv")
             eight(source_energy, UNROLL)
-            each(new_both, "start")
-        else:
-            each(old_both, "wait_recv")
-            eight(source_energy, UNROLL)
-            each(new_en, "start")
-            eight(source_speeds, UNROLL)
-            each(new_v0, "start")
-            each(rest, "start")
+            each(new_ens[0], "start")
 
         def azimuth_early(i, t, r):
             along_azimuth(f, i, t, r, EARLY)
 
-        eight(azimuth_early)
-
-        def inner_radius(n, _):
-            t, r = lax.div(n, 3), lax.rem(n, 3)
-            one = face(f, VR, (t + 1, r + 1), (t + 1, r + 2))
-            for q in range(5):
-                v = one(q)
-                flux[q, 4 * t + r] += v
-                flux[q, 4 * t + r + 1] -= v
-            return 0
-
-        lax.fori_loop(0, 6, inner_radius, 0)
-
-        def inner_theta(r, _):
-            one = face(f, VT, (1, r + 1), (2, r + 1))
-            for q in range(5):
-                v = one(q)
-                flux[q, r] += v
-                flux[q, 4 + r] -= v
-            return 0
-
-        lax.fori_loop(0, 4, inner_theta, 0)
-
-        each(news[step], "wait_recv")
-
-        for g, fields in ((1, LATE), (0, EARLY)) if last else ((0, (EN,)), (0, (VT, VR)), (1, LATE)):
-            if DE in fields:
-                each(lates[step], "wait_recv")
-            elif last:
-                each(new_both, "wait_recv")
-            else:
-                each(new_en if EN in fields else rest, "wait_recv")
+        def inner_faces(fields):
+            def inner_radius(n, _):
+                t, r = lax.div(n, 3), lax.rem(n, 3)
+                one = face(f, VR, (t + 1, r + 1), (t + 1, r + 2))
+                for q in fields:
+                    v = one(q)
+                    flux[q, 4 * t + r] += v
+                    flux[q, 4 * t + r + 1] -= v
+                return 0
+
+            lax.fori_loop(0, 6, inner_radius, 0)
+
+            def inner_theta(r, _):
+                one = face(f, VT, (1, r + 1), (2, r + 1))
+                for q in fields:
+                    v = one(q)
+                    flux[q, r] += v
+                    flux[q, 4 + r] -= v
+                return 0
+
+            lax.fori_loop(0, 4, inner_theta, 0)
+
+        inner_faces(LATE)
+        if not last:
+            eight(azimuth_early)
+            inner_faces(EARLY)
+        each(lates[step], "wait_recv")
+        all_beyond()
+
+        for g, fields in ((1, LATE), (0, EARLY)) if last else ((0, (VT, VR)), (0, (EN,)), (1, LATE)):
+            if last and EN in fields:
+                eight(azimuth_early)
+                inner_faces(EARLY)
+                each(rests[1], "wait_recv")
+                each(new_ens[1], "wait_recv")
+            elif not last and DE not in fields:
+                each(new_ens[0] if EN in fields else rests[0], "wait_recv")
 
             def outer_radius(t, _):
                 low = face(f, VR, (t + 1, 0), (t + 1, 1))
@@ -378,7 +445,7 @@
                         elif q == DE:
                             f1[F_AT[DE], t, r, pl.ds(8 * m, 8), :] = out
                         else:
-                            s1[S_AT[q], t, r, pl.ds(8 * m, 8), :] = out
+                            s1[S_AT[q], t + 1, r + 1, pl.ds(8 * m, 8), :] = out
 
             eight(rotate, UNROLL)
             if last:
@@ -386,9 +453,9 @@
                     to_blocks(k, g).start()
                 own_blocks(g).start()
             elif EN in fields:
-                each(old_en, "start")
+                each(olds_en[1], "start")
             elif VT in fields:
-                each(old_v, "start")
+                each(olds_v[1], "start")
             else:
                 begin(step + 1)
 
@@ -445,8 +512,8 @@
             pltpu.SMEM(fraction.shape, f32),
             pltpu.VMEM(block, f32),
             pltpu.VMEM((5, 256, 128), f32),
-            pltpu.VMEM((4, 4, 6, CHUNKS, 128), f32),
-            pltpu.VMEM((4, 4, 6, CHUNKS, 128), f32),
+            pltpu.VMEM((4, 6, 8, CHUNKS, 128), f32),
+            pltpu.VMEM((4, 6, 8, CHUNKS, 128), f32),
             pltpu.VMEM((5, 4, 6, CHUNKS, 128), f32),
             pltpu.VMEM((5, 4, 6, CHUNKS, 128), f32),
             pltpu.VMEM((8, CHUNKS, 128), f32),

time: 41.1 us -> 39.7 us (0.966)
  Pallas kernels: 40.3 us -> 38.9 us
    pallas_call x1, Pallas kernels: 39.4 us -> 38 us  [shards(): pl.pallas_call(kernel, out_shape=pltpu.VMEM(block, f32), in_specs=[hbm] *...]
where the time goes in v7:
time: 39.7 us; the launch traced here: 39.6 us
  Pallas kernels  38.9 us (98%)
  between operations  0.64 us (2%)
    pallas_call x1, Pallas kernels, shards(): pl.pallas_call(kernel, out_shape=pltpu.VMEM(block, f32), in_specs=[hbm] *...  38 us
    pallas_call x1, Pallas kernels, shards(): pl.pallas_call(write_out, out_shape=tuple((jax.ShapeDtypeStruct(v.shape,...  0.9 us

profile of v7, /device:TPU:1, one launch (start us, length us, event | category | flops | bytes accessed | tf_op | source)
XLA Modules:
  0.0 39.6 jit_solution(13012722896434212545)
XLA Ops:
  0.6 38.0 %shard_map.76.back = f32[16,5,16,128]{3,2,1,0:T(8,128)S(1)} custom-call(f32[16,8,256]{2,1,0:T(8,128)} %den_hbm.1, f32[3,16,8,256]{3,2,1,0:T(8,128)} %vel_hbm.1, f32[16,8,256]{2,1,0:T(8,128)} %ene_hbm.1, s32[8]{0:T(128)} %shift_hbm.1, f32[8]{0:T(128)} %frac_hbm.1), custom_call_target="tpu_custom_call" | custom-call | tf_op jit(solution)/shard_map/pallas_call | solution.py:505
  38.7 0.9 %shard_map.77 = (f32[16,8,256]{2,1,0:T(8,128)}, f32[3,16,8,256]{3,2,1,0:T(8,128)}, f32[16,8,256]{2,1,0:T(8,128)}) custom-call(f32[16,5,16,128]{3,2,1,0:T(8,128)S(1)} %shard_map.76.back), custom_call_target="tpu_custom_call" | custom-call | tf_op jit(solution)/shard_map/pallas_call | solution.py:536

commit v8 on v7

--- a/solution.py
+++ b/solution.py
@@ -113,7 +113,7 @@
                             ]
             return 0
 
-        lax.fori_loop(0, 8, one, 0)
+        lax.fori_loop(0, 8, one, 0, unroll=4)
 
     def to_rows(k, g):
         dest = peers[k]
@@ -222,7 +222,7 @@
                 else:
                     s0[S_AT[q], t + 1, r + 1] = value
 
-        eight(one)
+        eight(one, UNROLL)
 
     def to_blocks(k, g):
         dest = peers[k]

time: 39.7 us -> 39.6 us (level)
  no operation moved by 1% of the time
where the time goes in v8:
time: 39.6 us; the launch traced here: 39.4 us
  Pallas kernels  38.8 us (98%)
  between operations  0.64 us (2%)
    pallas_call x1, Pallas kernels, shards(): pl.pallas_call(kernel, out_shape=pltpu.VMEM(block, f32), in_specs=[hbm] *...  37.9 us
    pallas_call x1, Pallas kernels, shards(): pl.pallas_call(write_out, out_shape=tuple((jax.ShapeDtypeStruct(v.shape,...  0.9 us

profile of v8, /device:TPU:1, one launch (start us, length us, event | category | flops | bytes accessed | tf_op | source)
XLA Modules:
  0.0 39.4 jit_solution(18256082605427048932)
XLA Ops:
  0.6 37.9 %shard_map.76.back = f32[16,5,16,128]{3,2,1,0:T(8,128)S(1)} custom-call(f32[16,8,256]{2,1,0:T(8,128)} %den_hbm.1, f32[3,16,8,256]{3,2,1,0:T(8,128)} %vel_hbm.1, f32[16,8,256]{2,1,0:T(8,128)} %ene_hbm.1, s32[8]{0:T(128)} %shift_hbm.1, f32[8]{0:T(128)} %frac_hbm.1), custom_call_target="tpu_custom_call" | custom-call | tf_op jit(solution)/shard_map/pallas_call | solution.py:505
  38.5 0.9 %shard_map.77 = (f32[16,8,256]{2,1,0:T(8,128)}, f32[3,16,8,256]{3,2,1,0:T(8,128)}, f32[16,8,256]{2,1,0:T(8,128)}) custom-call(f32[16,5,16,128]{3,2,1,0:T(8,128)S(1)} %shard_map.76.back), custom_call_target="tpu_custom_call" | custom-call | tf_op jit(solution)/shard_map/pallas_call | solution.py:536

commit v9 on v8

--- a/solution.py
+++ b/solution.py
@@ -10,6 +10,7 @@
 QUADS = 32
 CHUNKS = 32
 CELLS = 4096
+PADDED = 264
 STEPS = 2
 
 EN, VT, VR, DE, VP = range(5)
@@ -126,6 +127,10 @@
             device_id_type=MESH,
         )
 
+    def whole_rows(g):
+        cells = rows.at[SPANS[g], pl.ds(0, 256), :]
+        return pltpu.make_async_copy(cells, cells, a_recv.at[g])
+
     def own_rows(g):
         return pltpu.make_async_copy(
             stage.at[a, SPANS[g]], rows.at[SPANS[g], pl.ds(pl.multiple_of(a * 16, 16), 16), :], a_recv.at[g]
@@ -281,11 +286,11 @@
         last = step == STEPS - 1
 
         if step == 0:
-            pltpu.make_async_copy(rows.at[SPANS[0]], rows.at[SPANS[0]], a_recv.at[0]).wait()
+            whole_rows(0).wait()
             unpack(EARLY)
             each(olds_en[0], "start")
             each(olds_v[0], "start")
-            pltpu.make_async_copy(rows.at[SPANS[1]], rows.at[SPANS[1]], a_recv.at[1]).wait()
+            whole_rows(1).wait()
             unpack(LATE)
             begin(0)
 
@@ -511,7 +516,7 @@
             pltpu.SMEM(shifts.shape, jnp.int32),
             pltpu.SMEM(fraction.shape, f32),
             pltpu.VMEM(block, f32),
-            pltpu.VMEM((5, 256, 128), f32),
+            pltpu.VMEM((5, PADDED, 128), f32),
             pltpu.VMEM((4, 6, 8, CHUNKS, 128), f32),
             pltpu.VMEM((4, 6, 8, CHUNKS, 128), f32),
             pltpu.VMEM((5, 4, 6, CHUNKS, 128), f32),
@@ -521,7 +526,7 @@
             pltpu.VMEM((8, CHUNKS, 128), f32),
             pltpu.VMEM((5, 8, CHUNKS, 128), f32),
             pltpu.VMEM((5, 8, 2 * CHUNKS, 128), f32),
-            pltpu.VMEM((5, 256, 128), f32),
+            pltpu.VMEM((5, PADDED, 128), f32),
             dma((2, AZ)),
             dma((2,)),
             dma((10, 4)),

time: 39.6 us -> 39.6 us (level)
  no operation moved by 1% of the time
where the time goes in v9:
time: 39.6 us; the launch traced here: 39.4 us
  Pallas kernels  38.8 us (98%)
  between operations  0.64 us (2%)
    pallas_call x1, Pallas kernels, shards(): pl.pallas_call(kernel, out_shape=pltpu.VMEM(block, f32), in_specs=[hbm] *...  37.9 us
    pallas_call x1, Pallas kernels, shards(): pl.pallas_call(write_out, out_shape=tuple((jax.ShapeDtypeStruct(v.shape,...  0.9 us

profile of v9, /device:TPU:1, one launch (start us, length us, event | category | flops | bytes accessed | tf_op | source)
XLA Modules:
  0.0 39.4 jit_solution(4100286587995596264)
XLA Ops:
  0.6 37.9 %shard_map.76.back = f32[16,5,16,128]{3,2,1,0:T(8,128)S(1)} custom-call(f32[16,8,256]{2,1,0:T(8,128)} %den_hbm.1, f32[3,16,8,256]{3,2,1,0:T(8,128)} %vel_hbm.1, f32[16,8,256]{2,1,0:T(8,128)} %ene_hbm.1, s32[8]{0:T(128)} %shift_hbm.1, f32[8]{0:T(128)} %frac_hbm.1), custom_call_target="tpu_custom_call" | custom-call | tf_op jit(solution)/shard_map/pallas_call | solution.py:510
  38.5 0.9 %shard_map.77 = (f32[16,8,256]{2,1,0:T(8,128)}, f32[3,16,8,256]{3,2,1,0:T(8,128)}, f32[16,8,256]{2,1,0:T(8,128)}) custom-call(f32[16,5,16,128]{3,2,1,0:T(8,128)S(1)} %shard_map.76.back), custom_call_target="tpu_custom_call" | custom-call | tf_op jit(solution)/shard_map/pallas_call | solution.py:541

commit v10 on v9

--- a/solution.py
+++ b/solution.py
@@ -393,11 +393,12 @@
         each(lates[step], "wait_recv")
         all_beyond()
 
-        for g, fields in ((1, LATE), (0, EARLY)) if last else ((0, (VT, VR)), (0, (EN,)), (1, LATE)):
-            if last and EN in fields:
+        for g, fields in ((1, LATE), (-1, (VT, VR)), (0, (EN,))) if last else ((0, (VT, VR)), (0, (EN,)), (1, LATE)):
+            if last and VT in fields:
                 eight(azimuth_early)
                 inner_faces(EARLY)
                 each(rests[1], "wait_recv")
+            elif last and EN in fields:
                 each(new_ens[1], "wait_recv")
             elif not last and DE not in fields:
                 each(new_ens[0] if EN in fields else rests[0], "wait_recv")
@@ -410,7 +411,7 @@
                     flux[q, 4 * t + 3] += high(q)
                 return 0
 
-            lax.fori_loop(0, 2, outer_radius, 0)
+            lax.fori_loop(0, 2, outer_radius, 0, unroll=2)
 
             def outer_theta(r, _):
                 low = face(f, VT, (0, r + 1), (1, r + 1))
@@ -420,7 +421,7 @@
                     flux[q, 4 + r] += high(q)
                 return 0
 
-            lax.fori_loop(0, 4, outer_theta, 0)
+            lax.fori_loop(0, 4, outer_theta, 0, unroll=4)
 
             def finish(i, t, r):
                 for q in fields:
@@ -453,10 +454,12 @@
                             s1[S_AT[q], t + 1, r + 1, pl.ds(8 * m, 8), :] = out
 
             eight(rotate, UNROLL)
-            if last:
+            if last and g >= 0:
                 for k in ORDER:
                     to_blocks(k, g).start()
                 own_blocks(g).start()
+            elif last:
+                pass
             elif EN in fields:
                 each(olds_en[1], "start")
             elif VT in fields:

time: 39.6 us -> 39.6 us (level)
  no operation moved by 1% of the time
where the time goes in v10:
time: 39.6 us; the launch traced here: 39.4 us
  Pallas kernels  38.8 us (98%)
  between operations  0.64 us (2%)
    pallas_call x1, Pallas kernels, shards(): pl.pallas_call(kernel, out_shape=pltpu.VMEM(block, f32), in_specs=[hbm] *...  37.9 us
    pallas_call x1, Pallas kernels, shards(): pl.pallas_call(write_out, out_shape=tuple((jax.ShapeDtypeStruct(v.shape,...  0.9 us

profile of v10, /device:TPU:1, one launch (start us, length us, event | category | flops | bytes accessed | tf_op | source)
XLA Modules:
  0.0 39.4 jit_solution(8385411703661754389)
XLA Ops:
  0.6 37.9 %shard_map.76.back = f32[16,5,16,128]{3,2,1,0:T(8,128)S(1)} custom-call(f32[16,8,256]{2,1,0:T(8,128)} %den_hbm.1, f32[3,16,8,256]{3,2,1,0:T(8,128)} %vel_hbm.1, f32[16,8,256]{2,1,0:T(8,128)} %ene_hbm.1, s32[8]{0:T(128)} %shift_hbm.1, f32[8]{0:T(128)} %frac_hbm.1), custom_call_target="tpu_custom_call" | custom-call | tf_op jit(solution)/shard_map/pallas_call | solution.py:513
  38.5 0.9 %shard_map.77 = (f32[16,8,256]{2,1,0:T(8,128)}, f32[3,16,8,256]{3,2,1,0:T(8,128)}, f32[16,8,256]{2,1,0:T(8,128)}) custom-call(f32[16,5,16,128]{3,2,1,0:T(8,128)S(1)} %shard_map.76.back), custom_call_target="tpu_custom_call" | custom-call | tf_op jit(solution)/shard_map/pallas_call | solution.py:544
